TPU v7x, 512 devices: a whole 4x4x16 slice. The times are simulated.
512 devices in a mesh: slab: 4 (over x_hi, core), energy: 128 (over y, z, x_lo).
Axes of the slice: x: 4 (x_hi: 2, x_lo: 2; x = x_hi * 2 + x_lo), y: 4, z: 16, core: 2. Of those that a mesh axis runs over, the one named last changes fastest.
Arguments:
- onsite: float32 [4, 384], P('slab'), may hold values from -1 to 1
- hopping: float32 [4, 384, 384], P('slab'), may hold values from -0.09 to 0.09, as said below
- separator_hamiltonian: float32 [128, 128], replicated, may hold values from -1 to 1, as said below
- coupling: float32 [4, 128], P('slab'), may hold values from 0.3 to 0.8
- bound_rows: int32 [4, 128], P('slab'), may hold values from 0 to 383, as said below
- old_sigma: float32 [2, 128, 4, 384, 384], P(None, 'energy', 'slab'), may hold values from -0.125 to 0.125
- phonon_vertex: float32 [4, 384, 384], P('slab'), may hold values from -0.3125 to 0.3125
- mode_steps: int32 [2], replicated, may hold values from 1 to 2, as said below
- mode_weights: float32 [2, 2], replicated, may hold values from 0.3 to 3
Outputs:
- new_sigma: float32 [2, 128, 4, 384, 384], P(None, 'energy', 'slab')
Inputs may be any that keep to these rules, and one draw needn't show every extreme that they name: Each slab's hopping block is symmetric with a zero diagonal. `separator_hamiltonian`: symmetric. `bound_rows`: each slab's 128 entries are distinct and ascending and include the slab's first and last orbital. `mode_steps`: the 2 modes have distinct steps.
All inputs are finite; a program needn't handle non-finite values.
Results may differ from a plain program's by a relative error of at most 0.0001.
Values sent between devices are 32-bit elements; how exact they have to be, the bound alone decides.
A program may use at most 192 MiB of HBM per device.

v0:
```python
import functools

import jax
import jax.numpy as jnp
from jax import lax
from jax.experimental import pallas as pl
from jax.experimental.pallas import tpu as pltpu
from jax.sharding import PartitionSpec as P

BROADENING = 1.0
LOWEST = -2.0
SPREAD = 4.0
CHUNK = 32
WINDOW = 3
LAG = 2
F32 = jnp.float32
BF16 = jnp.bfloat16


def split(x):
    high = x.astype(BF16)
    return high, (x - high.astype(F32)).astype(BF16)


def dot(x, y):
    return jnp.dot(x, y, preferred_element_type=F32)


def dot3(xh, xl, yh, yl):
    return dot(xh, yh) + dot(xh, yl) + dot(xl, yh)


def rot(p, b):
    r = (p.shape[1] - 2 * b) // 2
    parts = [-p[:, b : 2 * b], p[:, :b]]
    if r:
        parts += [-p[:, 2 * b + r :], p[:, 2 * b : 2 * b + r]]
    return jnp.concatenate(parts, axis=1)


def rot_rest(p):
    r = p.shape[1] // 2
    return jnp.concatenate([-p[:, r:], p[:, :r]], axis=1)


def iota(shape, axis):
    return lax.broadcasted_iota(jnp.int32, shape, axis)


def kernel(
    onsite_ref,
    hop_ref,
    ham_ref,
    cpl_ref,
    bound_ref,
    sigma_ref,
    vertex_ref,
    steps_ref,
    weights_ref,
    out_ref,
    khl,
    rhs,
    k2l,
    k4r,
    yv,
    yl,
    av,
    al,
    rr,
    vp,
    vt,
    q,
    acc,
    s_ref,
    r1_ref,
    h2_ref,
    r2_ref,
    f_ref,
    g_ref,
    x_ref,
    one_ref,
    sum_ref,
    got_ref,
    schur_send,
    schur_recv,
    x_send,
    x_recv,
    one_send,
    one_recv,
    sum_send,
    sum_recv,
):
    n = hop_ref.shape[-1]
    b = ham_ref.shape[0]
    r = n - b
    slab = lax.axis_index("slab")
    e = lax.axis_index("energy")
    energies = lax.axis_size("energy")
    core = lax.rem(slab, 2)
    other_core = slab + 1 - 2 * core
    other_chip = lax.rem(slab + 2, 4)
    odd = lax.rem(e, 2)
    pair = e + 1 - 2 * odd
    one_to = lax.rem(e - 2 + 4 * odd + energies, energies)
    sum_to = lax.rem(e + 2 - 4 * odd + energies, energies)

    barrier = pltpu.get_barrier_semaphore()
    for target in (
        {"slab": other_core},
        {"slab": other_chip},
        {"energy": pair},
        {"energy": one_to},
        {"energy": sum_to},
    ):
        pl.semaphore_signal(barrier, inc=1, device_id=target, device_id_type=pl.DeviceIdType.MESH)

    def remote(src, dst, send, recv, target):
        return pltpu.make_async_remote_copy(
            src_ref=src,
            dst_ref=dst,
            send_sem=send,
            recv_sem=recv,
            device_id=target,
            device_id_type=pl.DeviceIdType.MESH,
        )

    energy_value = LOWEST + SPREAD * (e.astype(F32) + 0.5) / energies

    eye_b = iota((b, b), 0) == iota((b, b), 1)
    bound_row = bound_ref[...]
    bound_col = jnp.sum(jnp.where(eye_b, bound_row, 0), axis=1, keepdims=True)
    here = iota((b, n), 1)
    count = jnp.sum(jnp.where(bound_col < here, 1, 0), axis=0, keepdims=True)
    is_bound = jnp.sum(jnp.where(bound_col == here, 1, 0), axis=0, keepdims=True)
    at = iota((1, n), 1)
    pos_row = jnp.where(is_bound > 0, count, b + at - count)
    here = iota((n, b), 0)
    count = jnp.sum(jnp.where(bound_row < here, 1, 0), axis=1, keepdims=True)
    is_bound = jnp.sum(jnp.where(bound_row == here, 1, 0), axis=1, keepdims=True)
    at = iota((n, 1), 0)
    pos_col = jnp.where(is_bound > 0, count, b + at - count)
    perm_mask = iota((n, n), 0) == pos_row
    perm = jnp.where(perm_mask, 1.0, 0.0).astype(BF16)
    perm_t = jnp.where(iota((n, n), 1) == pos_col, 1.0, 0.0).astype(BF16)

    eye = iota((n, n), 0) == iota((n, n), 1)
    sr = hop_ref[0] + sigma_ref[0, 0, 0]
    si = sigma_ref[1, 0, 0]
    dr = energy_value - onsite_ref[...] - jnp.sum(jnp.where(eye, sr, 0.0), axis=0, keepdims=True)
    di = BROADENING - jnp.sum(jnp.where(eye, si, 0.0), axis=0, keepdims=True)
    magnitude = dr * dr + di * di
    dr, di = dr / magnitude, -di / magnitude
    nr = jnp.where(eye, 0.0, -sr)
    ni = jnp.where(eye, 0.0, -si)
    krh, krl = split(nr * dr - ni * di)
    kih, kil = split(nr * di + ni * dr)
    moved = dot(perm, jnp.concatenate([krh, kih, krl, kil], axis=1)).astype(BF16)
    krh, kih, krl, kil = (dot(moved[:, i * n : (i + 1) * n], perm_t).astype(BF16) for i in range(4))
    dr_col = jnp.sum(jnp.where(perm_mask, dr, 0.0), axis=1, keepdims=True)
    di_col = jnp.sum(jnp.where(perm_mask, di, 0.0), axis=1, keepdims=True)

    def ordered(re, im):
        return jnp.concatenate([re[:, :b], im[:, :b], re[:, b:], im[:, b:]], axis=1)

    def store_rhs(ref, at, p, turned, columns):
        ref[at, 0:b, columns] = p[:b]
        ref[at, b : 2 * b, columns] = turned[:b]
        ref[at, 2 * b : 2 * b + r, columns] = p[b:]
        ref[at, 2 * b + r :, columns] = turned[b:]

    whole = slice(0, 2 * n)
    first = slice(0, 2 * b)
    rest = slice(2 * b, 2 * n)
    for i, p in enumerate((ordered(krh, kih), ordered(krl, kil))):
        khl[i] = p
        store_rhs(rhs, i, p, rot(p, b), whole)

    p = dot3(khl[0], khl[1], rhs[0], rhs[1])
    yv[...] = p
    for i, part in enumerate(split(p)):
        k2l[i] = part
        store_rhs(rhs, i, part, rot(part, b), whole)

    def identity(start, rows):
        row = iota((rows, 2 * n), 0) + start
        column = iota((rows, 2 * n), 1)
        orbital = jnp.where(column < b, column, jnp.where((column >= 2 * b) & (column < 2 * b + r), column - b, -1))
        return jnp.where(row == orbital, 1.0, 0.0)

    def y_rows(start, rows):
        at = slice(start, start + rows)
        k3 = dot3(khl[0, at], khl[1, at], rhs[0], rhs[1])
        u = identity(start, rows) - khl[0, at].astype(F32) - khl[1, at].astype(F32) + yv[at] - k3
        y = dr_col[at] * u + di_col[at] * rot(u, b)
        yv[at] = y
        for i, part in enumerate(split(y)):
            yl[i, at] = part

    def k4_columns(columns, turn):
        p = dot3(k2l[0], k2l[1], rhs[0, :, columns], rhs[1, :, columns])
        for i, part in enumerate(split(p)):
            store_rhs(k4r, i, part, turn(part), columns)

    y_rows(0, b)
    k4_columns(first, lambda part: rot(part, b))
    corner = yv[:b, first] + dot3(yl[0, :b], yl[1, :b], k4r[0, :, first], k4r[1, :, first])
    c_row = cpl_ref[...]
    c_col = jnp.sum(jnp.where(eye_b, c_row, 0.0), axis=1, keepdims=True)
    c_both = c_col * c_row
    s_ref[0] = corner[:, :b] * c_both
    s_ref[1] = corner[:, b:] * c_both

    pl.semaphore_wait(barrier, 5)
    step1 = remote(s_ref.at[1 - core], r1_ref, schur_send.at[0], schur_recv.at[0], {"slab": other_core})
    step1.start()
    y_rows(b, r)
    step1.wait()
    h2_ref[...] = s_ref[core] + r1_ref[...]
    step2 = remote(h2_ref, r2_ref, schur_send.at[1], schur_recv.at[1], {"slab": other_chip})
    step2.start()

    k4_columns(rest, rot_rest)
    a = yv[...] + dot3(yl[0], yl[1], k4r[0], k4r[1])
    av[...] = a
    for i, part in enumerate(split(a[:, first])):
        al[i] = part
    for i, part in enumerate(split(a[:b])):
        rr[i, :b] = part
        rr[i, b:] = rot(part, b)

    step2.wait()
    f_ref[core] = h2_ref[...] + r2_ref[...]
    step3 = remote(f_ref.at[core], f_ref.at[core], schur_send.at[2], schur_recv.at[2], {"slab": other_core})
    step3.start()
    for i, part in enumerate(split(vertex_ref[0])):
        v = dot(part, perm_t)
        vp[i] = v.astype(BF16)
        vt[i] = v.T.astype(BF16)
    step3.wait()

    tr = jnp.where(eye_b, 0.0, -ham_ref[...] - f_ref[0])
    ti = jnp.where(eye_b, 0.0, -f_ref[1])
    diag_r = jnp.where(eye_b, energy_value - ham_ref[...] - f_ref[0], 0.0)
    diag_i = jnp.where(eye_b, BROADENING - f_ref[1], 0.0)

    def reciprocal(axis):
        zr = jnp.sum(diag_r, axis=axis, keepdims=True)
        zi = jnp.sum(diag_i, axis=axis, keepdims=True)
        size = zr * zr + zi * zi
        return zr / size, -zi / size

    er, ei = reciprocal(0)
    er_col, ei_col = reciprocal(1)
    k = jnp.concatenate([tr * er - ti * ei, tr * ei + ti * er], axis=1)

    def turned(parts):
        return [jnp.concatenate([part, rot(part, b)], axis=0) for part in parts]

    one = jnp.where(iota((b, 2 * b), 0) == iota((b, 2 * b), 1), 1.0, 0.0)
    kl = split(k)
    k2 = dot3(*kl, *turned(kl))
    k2s = split(k2)
    k2t = turned(k2s)
    k3 = dot3(*kl, *k2t)
    k4 = dot3(*k2s, *k2t)
    u = one - k + k2 - k3
    u = er_col * u + ei_col * rot(u, b)
    t = u + dot3(*split(u), *turned(split(k4)))
    t = t * jnp.concatenate([c_both, c_both], axis=1)
    th, tl = turned(split(t))

    w = [[jnp.float32(0.0), jnp.float32(0.0)], [jnp.float32(0.0), jnp.float32(0.0)]]
    for way in range(2):
        for d in range(2):
            for m in range(2):
                w[way][d] = w[way][d] + jnp.where(steps_ref[m] == d + 1, weights_ref[way, m], 0.0)
    is_odd = odd == 1
    w_sum_own = jnp.where(is_odd, w[1][1], w[0][1])
    w_sum_pair = jnp.where(is_odd, w[1][0], w[0][0])
    w_pair = jnp.where(is_odd, w[0][0], w[1][0])
    one_from = e + 2 - 4 * odd
    sum_from = e - 2 + 4 * odd
    has_one = (one_from >= 0) & (one_from < energies)
    has_sum = (sum_from >= 0) & (sum_from < energies)
    w_one = jnp.where(is_odd, w[0][1], w[1][1])

    chunks = n // CHUNK
    started = []

    def x_copy(c):
        at = pl.ds(c * CHUNK, CHUNK)
        return remote(g_ref.at[at], x_ref.at[at], x_send.at[c], x_recv.at[c], {"energy": pair})

    def one_copy(c):
        at = pl.ds(c * CHUNK, CHUNK)
        return remote(g_ref.at[at], one_ref.at[at], one_send.at[c], one_recv.at[c], {"energy": one_to})

    def sum_copy(c):
        at = pl.ds(c * CHUNK, CHUNK)
        return remote(sum_ref.at[at], got_ref.at[at], sum_send.at[c], sum_recv.at[c], {"energy": sum_to})

    def send(c):
        x_copy(c).start()
        one_copy(c).start()

    for c in range(chunks):
        at = slice(c * CHUNK, (c + 1) * CHUNK)
        middle = dot3(al[0, at], al[1, at], th, tl)
        g_ref[at] = av[at] + dot3(*split(middle), rr[0], rr[1])
        if c < WINDOW:
            send(c)

    def mix(c):
        one_copy(c).wait_recv()
        sum_copy(c).wait_recv()
        at = slice(c * CHUNK, (c + 1) * CHUNK)
        mixed = w_pair * x_ref[at]
        mixed = mixed + jnp.where(has_one, w_one * one_ref[at], 0.0)
        mixed = mixed + jnp.where(has_sum, got_ref[at], 0.0)
        stacked = jnp.concatenate(
            [
                jnp.concatenate([mixed[:, :b], mixed[:, 2 * b : 2 * b + r]], axis=1),
                jnp.concatenate([mixed[:, b : 2 * b], mixed[:, 2 * b + r :]], axis=1),
            ],
            axis=0,
        )
        dressed = dot3(*split(stacked), vt[0], vt[1])
        for i, part in enumerate(split(dressed)):
            q[i, at, :n] = part[:CHUNK]
            q[i, at, n:] = part[CHUNK:]
        if (c + 1) * CHUNK == n - b:
            early = slice(0, n - b)
            acc[...] = dot3(vp[0, :, early], vp[1, :, early], q[0, early], q[1, early])

    for c in range(chunks + LAG):
        if c < chunks:
            x_copy(c).wait_recv()
            at = slice(c * CHUNK, (c + 1) * CHUNK)
            sum_ref[at] = w_sum_own * g_ref[at] + w_sum_pair * x_ref[at]
            sum_copy(c).start()
            if c + WINDOW < chunks:
                send(c + WINDOW)
        if c >= LAG:
            mix(c - LAG)

    late = slice(n - b, n)
    result = acc[...] + dot3(vp[0, :, late], vp[1, :, late], q[0, late], q[1, late])
    out_ref[0, 0, 0] = result[:, :n]
    out_ref[1, 0, 0] = result[:, n:]
    for c in range(chunks):
        x_copy(c).wait_send()
        one_copy(c).wait_send()
        sum_copy(c).wait_send()


def per_device(*arrays):
    n = arrays[1].shape[-1]
    b = arrays[2].shape[0]
    chunks = n // CHUNK
    vmem = pl.BlockSpec(memory_space=pltpu.VMEM)
    smem = pl.BlockSpec(memory_space=pltpu.SMEM)
    dma = pltpu.SemaphoreType.DMA
    return pl.pallas_call(
        kernel,
        out_shape=jax.ShapeDtypeStruct(arrays[5].shape, F32),
        in_specs=[vmem] * 7 + [smem] * 2,
        out_specs=vmem,
        scratch_shapes=[
            pltpu.VMEM((2, n, 2 * n), BF16),
            pltpu.VMEM((2, 2 * n, 2 * n), BF16),
            pltpu.VMEM((2, n, 2 * n), BF16),
            pltpu.VMEM((2, 2 * n, 2 * n), BF16),
            pltpu.VMEM((n, 2 * n), F32),
            pltpu.VMEM((2, n, 2 * n), BF16),
            pltpu.VMEM((n, 2 * n), F32),
            pltpu.VMEM((2, n, 2 * b), BF16),
            pltpu.VMEM((2, 2 * b, 2 * n), BF16),
            pltpu.VMEM((2, n, n), BF16),
            pltpu.VMEM((2, n, n), BF16),
            pltpu.VMEM((2, n, 2 * n), BF16),
            pltpu.VMEM((n, 2 * n), F32),
            pltpu.VMEM((2, b, b), F32),
            pltpu.VMEM((b, b), F32),
            pltpu.VMEM((b, b), F32),
            pltpu.VMEM((b, b), F32),
            pltpu.VMEM((2, b, b), F32),
            pltpu.VMEM((n, 2 * n), F32),
            pltpu.VMEM((n, 2 * n), F32),
            pltpu.VMEM((n, 2 * n), F32),
            pltpu.VMEM((n, 2 * n), F32),
            pltpu.VMEM((n, 2 * n), F32),
            dma((3,)),
            dma((3,)),
            dma((chunks,)),
            dma((chunks,)),
            dma((chunks,)),
            dma((chunks,)),
            dma((chunks,)),
            dma((chunks,)),
        ],
        compiler_params=pltpu.CompilerParams(
            collective_id=0, has_side_effects=True, vmem_limit_bytes=52 * 2**20
        ),
    )(*arrays)


def solution(mesh):
    placed = (
        P("slab", None),
        P("slab", None, None),
        P(),
        P("slab", None),
        P("slab", None),
        P(None, "energy", "slab", None, None),
        P("slab", None, None),
        P(),
        P(),
    )
    return jax.shard_map(
        per_device,
        mesh=mesh,
        in_specs=placed,
        out_specs=P(None, "energy", "slab", None, None),
        check_vma=False,
    )
```

profile of v0, /device:TPU:1, one launch (start us, length us, event | category | flops | bytes accessed | tf_op | source)
XLA Modules:
  0.0 75.7 jit_solution(13791948005339881449)
XLA Ops:
  0.0 0.0 copy-start
  0.0 1.1 %copy-done = f32[1,384,384]{2,1,0:T(8,128)S(1)} copy-done((f32[1,384,384]{2,1,0:T(8,128)S(1)}, f32[1,384,384]{2,1,0:T(8,128)}, u32[]{:S(2)}) %copy-start) | copy-done | bytes 589848
  1.1 0.0 copy-start.1
  1.1 1.1 %copy-done.1 = f32[1,384,384]{2,1,0:T(8,128)S(1)} copy-done((f32[1,384,384]{2,1,0:T(8,128)S(1)}, f32[1,384,384]{2,1,0:T(8,128)}, u32[]{:S(2)}) %copy-start.1) | copy-done | bytes 589848
  2.1 0.0 copy-start.2
  2.1 0.8 %copy-done.2 = f32[128,128]{1,0:T(8,128)S(1)} copy-done((f32[128,128]{1,0:T(8,128)S(1)}, f32[128,128]{1,0:T(8,128)}, u32[]{:S(2)}) %copy-start.2) | copy-done | bytes 65560
  3.0 0.0 copy-start.3
  3.0 0.7 copy-done.3
  3.7 0.0 copy-start.4
  3.7 0.7 copy-done.4
  4.3 0.0 copy-start.5
  4.3 0.7 copy-done.5
  5.0 0.0 copy-start.6
  5.0 0.7 copy-done.6
  5.6 0.0 copy-start.7
  5.6 0.7 copy-done.7
  6.3 67.0 %shard_map.91 = f32[2,1,1,384,384]{4,3,2,1,0:T(8,128)} custom-call(f32[1,384]{1,0:T(1,128)S(1)} %copy-done.3, f32[1,384,384]{2,1,0:T(8,128)S(1)} %copy-done, f32[128,128]{1,0:T(8,128)S(1)} %copy-done.2, f32[1,128]{1,0:T(1,128)S(1)} %copy-done.5, s32[1,128]{1,0:T(1,128)S(1)} %copy-done.6, f32[2,1,1,384,384]{4,3,2,1,0:T(8,128)} %sigma_ref.1, ...), custom_call_target="tpu_custom_call" | custom-call | tf_op jit(solution)/shard_map/pallas_call | solution.py:363
  73.3 2.4 %copy.11 = f32[2,1,1,384,384]{4,3,2,1,0:T(8,128)} copy(f32[2,1,1,384,384]{4,3,2,1,0:T(8,128)} %shard_map.91) | data formatting | bytes 2359296
Async XLA Ops:
  0.0 1.1 %copy-start = (f32[1,384,384]{2,1,0:T(8,128)S(1)}, f32[1,384,384]{2,1,0:T(8,128)}, u32[]{:S(2)}) copy-start(f32[1,384,384]{2,1,0:T(8,128)} %hop_ref.1) | copy-start | bytes 1769476
  1.1 1.1 %copy-start.1 = (f32[1,384,384]{2,1,0:T(8,128)S(1)}, f32[1,384,384]{2,1,0:T(8,128)}, u32[]{:S(2)}) copy-start(f32[1,384,384]{2,1,0:T(8,128)} %vertex_ref.1) | copy-start | bytes 1769476
  2.1 0.8 %copy-start.2 = (f32[128,128]{1,0:T(8,128)S(1)}, f32[128,128]{1,0:T(8,128)}, u32[]{:S(2)}) copy-start(f32[128,128]{1,0:T(8,128)} %ham_ref.1) | copy-start | bytes 196612
  3.0 0.7 copy-start.3
  3.7 0.7 copy-start.4
  4.3 0.7 copy-start.5
  5.0 0.7 copy-start.6
  5.6 0.7 copy-start.7
where the time goes:
time: 76 us; the launch traced here: 75.7 us
  Pallas kernels  67 us (88%)
  local copies, waits for them, and re-layouts  8.65 us (11%)
    pallas_call x1, Pallas kernels, per_device(): pl.pallas_call(kernel, out_shape=jax.ShapeDtypeStruct(arrays[5].shape, F3...  67 us
    unnamed x17, local copies, waits for them, and re-layouts  8.65 us

commit v1 on v0

--- a/solution.py
+++ b/solution.py
@@ -13,6 +13,7 @@
 CHUNK = 32
 WINDOW = 3
 LAG = 2
+GROUPS = (32, 96, 256)
 F32 = jnp.float32
 BF16 = jnp.bfloat16
 
@@ -48,6 +49,16 @@
 
 
 def kernel(
+    onsite_in,
+    hop_in,
+    ham_in,
+    cpl_in,
+    bound_in,
+    sigma_in,
+    vertex_in,
+    steps_ref,
+    weights_ref,
+    out_ref,
     onsite_ref,
     hop_ref,
     ham_ref,
@@ -55,9 +66,9 @@
     bound_ref,
     sigma_ref,
     vertex_ref,
-    steps_ref,
-    weights_ref,
-    out_ref,
+    res_ref,
+    in_sem,
+    out_sem,
     khl,
     rhs,
     k2l,
@@ -71,6 +82,7 @@
     vt,
     q,
     acc,
+    th_ref,
     s_ref,
     r1_ref,
     h2_ref,
@@ -104,6 +116,22 @@
     one_to = lax.rem(e - 2 + 4 * odd + energies, energies)
     sum_to = lax.rem(e + 2 - 4 * odd + energies, energies)
 
+    loads = [
+        pltpu.make_async_copy(src, dst, in_sem.at[i])
+        for i, (src, dst) in enumerate(
+            (
+                (bound_in, bound_ref),
+                (sigma_in, sigma_ref),
+                (hop_in, hop_ref),
+                (onsite_in, onsite_ref),
+                (cpl_in, cpl_ref),
+                (ham_in, ham_ref),
+                (vertex_in, vertex_ref),
+            )
+        )
+    ]
+    for load in loads[:5]:
+        load.start()
     barrier = pltpu.get_barrier_semaphore()
     for target in (
         {"slab": other_core},
@@ -124,8 +152,12 @@
             device_id_type=pl.DeviceIdType.MESH,
         )
 
+    def apart(work):
+        pl.when(slab >= 0)(work)
+
     energy_value = LOWEST + SPREAD * (e.astype(F32) + 0.5) / energies
 
+    loads[0].wait()
     eye_b = iota((b, b), 0) == iota((b, b), 1)
     bound_row = bound_ref[...]
     bound_col = jnp.sum(jnp.where(eye_b, bound_row, 0), axis=1, keepdims=True)
@@ -143,6 +175,10 @@
     perm = jnp.where(perm_mask, 1.0, 0.0).astype(BF16)
     perm_t = jnp.where(iota((n, n), 1) == pos_col, 1.0, 0.0).astype(BF16)
 
+    for load in loads[1:4]:
+        load.wait()
+    for load in loads[5:]:
+        load.start()
     eye = iota((n, n), 0) == iota((n, n), 1)
     sr = hop_ref[0] + sigma_ref[0, 0, 0]
     si = sigma_ref[1, 0, 0]
@@ -156,8 +192,16 @@
     kih, kil = split(nr * di + ni * dr)
     moved = dot(perm, jnp.concatenate([krh, kih, krl, kil], axis=1)).astype(BF16)
     krh, kih, krl, kil = (dot(moved[:, i * n : (i + 1) * n], perm_t).astype(BF16) for i in range(4))
-    dr_col = jnp.sum(jnp.where(perm_mask, dr, 0.0), axis=1, keepdims=True)
-    di_col = jnp.sum(jnp.where(perm_mask, di, 0.0), axis=1, keepdims=True)
+    rows = iota((8, n), 0)
+    pieces = jnp.zeros((8, n), F32)
+    for i, d in enumerate((dr, di)):
+        for j in range(3):
+            part = d.astype(BF16).astype(F32)
+            pieces = jnp.where(rows == 3 * i + j, part, pieces)
+            d = d - part
+    pieces = dot(pieces.astype(BF16), perm_t).T
+    dr_col = pieces[:, 0:1] + pieces[:, 1:2] + pieces[:, 2:3]
+    di_col = pieces[:, 3:4] + pieces[:, 4:5] + pieces[:, 5:6]
 
     def ordered(re, im):
         return jnp.concatenate([re[:, :b], im[:, :b], re[:, b:], im[:, b:]], axis=1)
@@ -204,6 +248,7 @@
     y_rows(0, b)
     k4_columns(first, lambda part: rot(part, b))
     corner = yv[:b, first] + dot3(yl[0, :b], yl[1, :b], k4r[0, :, first], k4r[1, :, first])
+    loads[4].wait()
     c_row = cpl_ref[...]
     c_col = jnp.sum(jnp.where(eye_b, c_row, 0.0), axis=1, keepdims=True)
     c_both = c_col * c_row
@@ -213,29 +258,38 @@
     pl.semaphore_wait(barrier, 5)
     step1 = remote(s_ref.at[1 - core], r1_ref, schur_send.at[0], schur_recv.at[0], {"slab": other_core})
     step1.start()
-    y_rows(b, r)
+    apart(lambda: y_rows(b, r))
     step1.wait()
     h2_ref[...] = s_ref[core] + r1_ref[...]
     step2 = remote(h2_ref, r2_ref, schur_send.at[1], schur_recv.at[1], {"slab": other_chip})
     step2.start()
 
-    k4_columns(rest, rot_rest)
-    a = yv[...] + dot3(yl[0], yl[1], k4r[0], k4r[1])
-    av[...] = a
-    for i, part in enumerate(split(a[:, first])):
-        al[i] = part
-    for i, part in enumerate(split(a[:b])):
-        rr[i, :b] = part
-        rr[i, b:] = rot(part, b)
+    def finish_inverse():
+        k4_columns(rest, rot_rest)
+        a = yv[...] + dot3(yl[0], yl[1], k4r[0], k4r[1])
+        av[...] = a
+        for i, part in enumerate(split(a[:, first])):
+            al[i] = part
+        for i, part in enumerate(split(a[:b])):
+            rr[i, :b] = part
+            rr[i, b:] = rot(part, b)
+
+    apart(finish_inverse)
 
     step2.wait()
     f_ref[core] = h2_ref[...] + r2_ref[...]
     step3 = remote(f_ref.at[core], f_ref.at[core], schur_send.at[2], schur_recv.at[2], {"slab": other_core})
     step3.start()
-    for i, part in enumerate(split(vertex_ref[0])):
-        v = dot(part, perm_t)
-        vp[i] = v.astype(BF16)
-        vt[i] = v.T.astype(BF16)
+    loads[5].wait()
+    loads[6].wait()
+
+    def order_vertex():
+        for i, part in enumerate(split(vertex_ref[0])):
+            v = dot(part, perm_t)
+            vp[i] = v.astype(BF16)
+            vt[i] = v.T.astype(BF16)
+
+    apart(order_vertex)
     step3.wait()
 
     tr = jnp.where(eye_b, 0.0, -ham_ref[...] - f_ref[0])
@@ -303,16 +357,21 @@
         x_copy(c).start()
         one_copy(c).start()
 
-    for c in range(chunks):
-        at = slice(c * CHUNK, (c + 1) * CHUNK)
-        middle = dot3(al[0, at], al[1, at], th, tl)
+    th_ref[0], th_ref[1] = th, tl
+
+    def greens(start, rows):
+        at = slice(start, start + rows)
+        middle = dot3(al[0, at], al[1, at], th_ref[0], th_ref[1])
         g_ref[at] = av[at] + dot3(*split(middle), rr[0], rr[1])
-        if c < WINDOW:
+
+    start = 0
+    for rows in GROUPS:
+        apart(functools.partial(greens, start, rows))
+        for c in range(start // CHUNK, min((start + rows) // CHUNK, WINDOW)):
             send(c)
+        start += rows
 
     def mix(c):
-        one_copy(c).wait_recv()
-        sum_copy(c).wait_recv()
         at = slice(c * CHUNK, (c + 1) * CHUNK)
         mixed = w_pair * x_ref[at]
         mixed = mixed + jnp.where(has_one, w_one * one_ref[at], 0.0)
@@ -341,31 +400,43 @@
             if c + WINDOW < chunks:
                 send(c + WINDOW)
         if c >= LAG:
-            mix(c - LAG)
+            one_copy(c - LAG).wait_recv()
+            sum_copy(c - LAG).wait_recv()
+            apart(functools.partial(mix, c - LAG))
 
     late = slice(n - b, n)
-    result = acc[...] + dot3(vp[0, :, late], vp[1, :, late], q[0, late], q[1, late])
-    out_ref[0, 0, 0] = result[:, :n]
-    out_ref[1, 0, 0] = result[:, n:]
+    stores = []
+    for i in range(2):
+        half = slice(i * n, (i + 1) * n)
+        res_ref[i] = acc[:, half] + dot3(vp[0, :, late], vp[1, :, late], q[0, late, half], q[1, late, half])
+        store = pltpu.make_async_copy(res_ref.at[i], out_ref.at[i, 0, 0], out_sem.at[i])
+        store.start()
+        stores.append(store)
     for c in range(chunks):
         x_copy(c).wait_send()
         one_copy(c).wait_send()
         sum_copy(c).wait_send()
+    for store in stores:
+        store.wait()
 
 
 def per_device(*arrays):
     n = arrays[1].shape[-1]
     b = arrays[2].shape[0]
     chunks = n // CHUNK
-    vmem = pl.BlockSpec(memory_space=pltpu.VMEM)
+    hbm = pl.BlockSpec(memory_space=pl.ANY)
     smem = pl.BlockSpec(memory_space=pltpu.SMEM)
     dma = pltpu.SemaphoreType.DMA
     return pl.pallas_call(
         kernel,
         out_shape=jax.ShapeDtypeStruct(arrays[5].shape, F32),
-        in_specs=[vmem] * 7 + [smem] * 2,
-        out_specs=vmem,
+        in_specs=[hbm] * 7 + [smem] * 2,
+        out_specs=hbm,
         scratch_shapes=[
+            *(pltpu.VMEM(a.shape, a.dtype) for a in arrays[:7]),
+            pltpu.VMEM((2, n, n), F32),
+            dma((7,)),
+            dma((2,)),
             pltpu.VMEM((2, n, 2 * n), BF16),
             pltpu.VMEM((2, 2 * n, 2 * n), BF16),
             pltpu.VMEM((2, n, 2 * n), BF16),
@@ -379,6 +450,7 @@
             pltpu.VMEM((2, n, n), BF16),
             pltpu.VMEM((2, n, 2 * n), BF16),
             pltpu.VMEM((n, 2 * n), F32),
+            pltpu.VMEM((2, 2 * b, 2 * b), BF16),
             pltpu.VMEM((2, b, b), F32),
             pltpu.VMEM((b, b), F32),
             pltpu.VMEM((b, b), F32),
@@ -399,7 +471,7 @@
             dma((chunks,)),
         ],
         compiler_params=pltpu.CompilerParams(
-            collective_id=0, has_side_effects=True, vmem_limit_bytes=52 * 2**20
+            collective_id=0, has_side_effects=True, vmem_limit_bytes=60 * 2**20
         ),
     )(*arrays)
 

time: 76 us -> 64.5 us (0.85)
  local copies, waits for them, and re-layouts: 8.65 us -> 2.36 us
  Pallas kernels: 67 us -> 61.9 us
    unnamed x17 -> x1, local copies, waits for them, and re-layouts: 8.65 us -> 2.36 us
    pallas_call x1, Pallas kernels: 67 us -> 61.9 us  [per_device(): pl.pallas_call(kernel, out_shape=jax.ShapeDtypeStruct(arrays[5].shape, F3...]
where the time goes in v1:
time: 64.5 us; the launch traced here: 64.3 us
  Pallas kernels  61.9 us (96%)
  local copies, waits for them, and re-layouts  2.36 us (4%)
    pallas_call x1, Pallas kernels, per_device(): pl.pallas_call(kernel, out_shape=jax.ShapeDtypeStruct(arrays[5].shape, F3...  61.9 us
    unnamed x1, local copies, waits for them, and re-layouts  2.36 us

profile of v1, /device:TPU:1, one launch (start us, length us, event | category | flops | bytes accessed | tf_op | source)
XLA Modules:
  0.0 64.3 jit_solution(12237751794389446192)
XLA Ops:
  0.0 61.9 %shard_map.91 = f32[2,1,1,384,384]{4,3,2,1,0:T(8,128)} custom-call(f32[1,384]{1,0:T(1,128)} %onsite_in.1, f32[1,384,384]{2,1,0:T(8,128)} %hop_in.1, f32[128,128]{1,0:T(8,128)} %ham_in.1, f32[1,128]{1,0:T(1,128)} %cpl_in.1, s32[1,128]{1,0:T(1,128)} %bound_in.1, f32[2,1,1,384,384]{4,3,2,1,0:T(8,128)} %sigma_in.1, f32[1,384,384]{2,1,0:T(8,128)} %vertex_in.1, ...), custom_call_target="tpu_custom_call" | custom-call | tf_op jit(solution)/shard_map/pallas_call | solution.py:430
  61.9 2.4 %copy.11 = f32[2,1,1,384,384]{4,3,2,1,0:T(8,128)} copy(f32[2,1,1,384,384]{4,3,2,1,0:T(8,128)} %shard_map.91) | data formatting | bytes 2359296

commit v2 on v1

--- a/solution.py
+++ b/solution.py
@@ -11,6 +11,9 @@
 LOWEST = -2.0
 SPREAD = 4.0
 CHUNK = 32
+MIX = 32
+ONE = 128
+PART = 32
 WINDOW = 3
 LAG = 2
 GROUPS = (32, 96, 256)
@@ -28,7 +31,7 @@
 
 
 def dot3(xh, xl, yh, yl):
-    return dot(xh, yh) + dot(xh, yl) + dot(xl, yh)
+    return dot(jnp.concatenate([xh, xh, xl], axis=1), jnp.concatenate([yh, yl, yh], axis=0))
 
 
 def rot(p, b):
@@ -113,8 +116,12 @@
     other_chip = lax.rem(slab + 2, 4)
     odd = lax.rem(e, 2)
     pair = e + 1 - 2 * odd
-    one_to = lax.rem(e - 2 + 4 * odd + energies, energies)
-    sum_to = lax.rem(e + 2 - 4 * odd + energies, energies)
+    one_to = e - 2 + 4 * odd
+    sum_to = e + 2 - 4 * odd
+    ahead = (one_to >= 0) & (one_to < energies)
+    behind = (sum_to >= 0) & (sum_to < energies)
+    one_to = lax.rem(one_to + energies, energies)
+    sum_to = lax.rem(sum_to + energies, energies)
 
     loads = [
         pltpu.make_async_copy(src, dst, in_sem.at[i])
@@ -133,14 +140,15 @@
     for load in loads[:5]:
         load.start()
     barrier = pltpu.get_barrier_semaphore()
-    for target in (
-        {"slab": other_core},
-        {"slab": other_chip},
-        {"energy": pair},
-        {"energy": one_to},
-        {"energy": sum_to},
-    ):
+
+    def greet(target):
         pl.semaphore_signal(barrier, inc=1, device_id=target, device_id_type=pl.DeviceIdType.MESH)
+
+    greet({"slab": other_core})
+    greet({"slab": other_chip})
+    greet({"energy": pair})
+    pl.when(ahead)(lambda: greet({"energy": one_to}))
+    pl.when(behind)(lambda: greet({"energy": sum_to}))
 
     def remote(src, dst, send, recv, target):
         return pltpu.make_async_remote_copy(
@@ -245,8 +253,13 @@
         for i, part in enumerate(split(p)):
             store_rhs(k4r, i, part, turn(part), columns)
 
+    def k4_columns(columns, turn):
+        p = dot3(k2l[0], k2l[1], rhs[0, :, columns], rhs[1, :, columns])
+        for i, part in enumerate(split(p)):
+            store_rhs(k4r, i, part, turn(part), columns)
+
+    k4_columns(first, lambda part: rot(part, b))
     y_rows(0, b)
-    k4_columns(first, lambda part: rot(part, b))
     corner = yv[:b, first] + dot3(yl[0, :b], yl[1, :b], k4r[0, :, first], k4r[1, :, first])
     loads[4].wait()
     c_row = cpl_ref[...]
@@ -255,17 +268,20 @@
     s_ref[0] = corner[:, :b] * c_both
     s_ref[1] = corner[:, b:] * c_both
 
-    pl.semaphore_wait(barrier, 5)
+    pl.semaphore_wait(barrier, 3 + ahead.astype(jnp.int32) + behind.astype(jnp.int32))
     step1 = remote(s_ref.at[1 - core], r1_ref, schur_send.at[0], schur_recv.at[0], {"slab": other_core})
     step1.start()
-    apart(lambda: y_rows(b, r))
+    @apart
+    def _():
+        k4_columns(rest, rot_rest)
+
     step1.wait()
     h2_ref[...] = s_ref[core] + r1_ref[...]
     step2 = remote(h2_ref, r2_ref, schur_send.at[1], schur_recv.at[1], {"slab": other_chip})
     step2.start()
 
     def finish_inverse():
-        k4_columns(rest, rot_rest)
+        y_rows(b, r)
         a = yv[...] + dot3(yl[0], yl[1], k4r[0], k4r[1])
         av[...] = a
         for i, part in enumerate(split(a[:, first])):
@@ -332,30 +348,27 @@
     w_sum_own = jnp.where(is_odd, w[1][1], w[0][1])
     w_sum_pair = jnp.where(is_odd, w[1][0], w[0][0])
     w_pair = jnp.where(is_odd, w[0][0], w[1][0])
-    one_from = e + 2 - 4 * odd
-    sum_from = e - 2 + 4 * odd
-    has_one = (one_from >= 0) & (one_from < energies)
-    has_sum = (sum_from >= 0) & (sum_from < energies)
     w_one = jnp.where(is_odd, w[0][1], w[1][1])
 
     chunks = n // CHUNK
-    started = []
-
-    def x_copy(c):
-        at = pl.ds(c * CHUNK, CHUNK)
-        return remote(g_ref.at[at], x_ref.at[at], x_send.at[c], x_recv.at[c], {"energy": pair})
-
-    def one_copy(c):
-        at = pl.ds(c * CHUNK, CHUNK)
-        return remote(g_ref.at[at], one_ref.at[at], one_send.at[c], one_recv.at[c], {"energy": one_to})
-
-    def sum_copy(c):
-        at = pl.ds(c * CHUNK, CHUNK)
-        return remote(sum_ref.at[at], got_ref.at[at], sum_send.at[c], sum_recv.at[c], {"energy": sum_to})
+    def x_copy(at, c):
+        return remote(g_ref.at[at], x_ref.at[at], x_send, x_recv.at[c], {"energy": pair})
+
+    def one_copy(at, c):
+        return remote(g_ref.at[at], one_ref.at[at], one_send, one_recv.at[c], {"energy": one_to})
+
+    def sum_copy(at, c):
+        return remote(sum_ref.at[at], got_ref.at[at], sum_send, sum_recv.at[c], {"energy": sum_to})
+
+    def rows_of(c, size=CHUNK):
+        return pl.ds(c * size, size)
 
     def send(c):
-        x_copy(c).start()
-        one_copy(c).start()
+        x_copy(rows_of(c), c).start()
+        end = (c + 1) * CHUNK
+        if end % PART == 0:
+            at = pl.ds(end - PART, PART)
+            pl.when(ahead)(lambda: one_copy(at, (end - 1) // ONE).start())
 
     th_ref[0], th_ref[1] = th, tl
 
@@ -371,11 +384,11 @@
             send(c)
         start += rows
 
-    def mix(c):
-        at = slice(c * CHUNK, (c + 1) * CHUNK)
+    def mix(start):
+        at = slice(start, start + MIX)
         mixed = w_pair * x_ref[at]
-        mixed = mixed + jnp.where(has_one, w_one * one_ref[at], 0.0)
-        mixed = mixed + jnp.where(has_sum, got_ref[at], 0.0)
+        mixed = mixed + jnp.where(behind, w_one * one_ref[at], 0.0)
+        mixed = mixed + jnp.where(ahead, got_ref[at], 0.0)
         stacked = jnp.concatenate(
             [
                 jnp.concatenate([mixed[:, :b], mixed[:, 2 * b : 2 * b + r]], axis=1),
@@ -385,25 +398,28 @@
         )
         dressed = dot3(*split(stacked), vt[0], vt[1])
         for i, part in enumerate(split(dressed)):
-            q[i, at, :n] = part[:CHUNK]
-            q[i, at, n:] = part[CHUNK:]
-        if (c + 1) * CHUNK == n - b:
+            q[i, at, :n] = part[:MIX]
+            q[i, at, n:] = part[MIX:]
+        if start + MIX == n - b:
             early = slice(0, n - b)
             acc[...] = dot3(vp[0, :, early], vp[1, :, early], q[0, early], q[1, early])
 
     for c in range(chunks + LAG):
         if c < chunks:
-            x_copy(c).wait_recv()
+            x_copy(rows_of(c), c).wait_recv()
             at = slice(c * CHUNK, (c + 1) * CHUNK)
             sum_ref[at] = w_sum_own * g_ref[at] + w_sum_pair * x_ref[at]
-            sum_copy(c).start()
+            pl.when(behind)(lambda: sum_copy(rows_of(c), c).start())
             if c + WINDOW < chunks:
                 send(c + WINDOW)
         if c >= LAG:
-            one_copy(c - LAG).wait_recv()
-            sum_copy(c - LAG).wait_recv()
-            apart(functools.partial(mix, c - LAG))
-
+            done = c - LAG
+            if done * CHUNK % ONE == 0:
+                at = done * CHUNK // ONE
+                pl.when(behind)(lambda: one_copy(rows_of(at, ONE), at).wait_recv())
+            pl.when(ahead)(lambda: sum_copy(rows_of(done), done).wait_recv())
+            if (done + 1) * CHUNK % MIX == 0:
+                apart(functools.partial(mix, (done + 1) * CHUNK - MIX))
     late = slice(n - b, n)
     stores = []
     for i in range(2):
@@ -412,10 +428,10 @@
         store = pltpu.make_async_copy(res_ref.at[i], out_ref.at[i, 0, 0], out_sem.at[i])
         store.start()
         stores.append(store)
-    for c in range(chunks):
-        x_copy(c).wait_send()
-        one_copy(c).wait_send()
-        sum_copy(c).wait_send()
+    every = pl.ds(0, n)
+    x_copy(every, 0).wait_send()
+    pl.when(ahead)(lambda: one_copy(every, 0).wait_send())
+    pl.when(behind)(lambda: sum_copy(every, 0).wait_send())
     for store in stores:
         store.wait()
 
@@ -463,11 +479,11 @@
             pltpu.VMEM((n, 2 * n), F32),
             dma((3,)),
             dma((3,)),
+            dma,
             dma((chunks,)),
-            dma((chunks,)),
-            dma((chunks,)),
-            dma((chunks,)),
-            dma((chunks,)),
+            dma,
+            dma((n // ONE,)),
+            dma,
             dma((chunks,)),
         ],
         compiler_params=pltpu.CompilerParams(

time: 64.5 us -> 61.2 us (0.949)
  the two profiles are of different devices: /device:TPU:1 before, /device:TPU:24 now
where the time goes in v2:
time: 61.2 us; the launch traced here: 61.1 us
  Pallas kernels  58.7 us (96%)
  local copies, waits for them, and re-layouts  2.36 us (4%)
    pallas_call x1, Pallas kernels, per_device(): pl.pallas_call(kernel, out_shape=jax.ShapeDtypeStruct(arrays[5].shape, F3...  58.7 us
    unnamed x1, local copies, waits for them, and re-layouts  2.36 us

profile of v2, /device:TPU:24, one launch (start us, length us, event | category | flops | bytes accessed | tf_op | source)
XLA Modules:
  0.0 61.1 jit_solution(16644578307625538432)
XLA Ops:
  0.0 58.7 %shard_map.91 = f32[2,1,1,384,384]{4,3,2,1,0:T(8,128)} custom-call(f32[1,384]{1,0:T(1,128)} %onsite_in.1, f32[1,384,384]{2,1,0:T(8,128)} %hop_in.1, f32[128,128]{1,0:T(8,128)} %ham_in.1, f32[1,128]{1,0:T(1,128)} %cpl_in.1, s32[1,128]{1,0:T(1,128)} %bound_in.1, f32[2,1,1,384,384]{4,3,2,1,0:T(8,128)} %sigma_in.1, f32[1,384,384]{2,1,0:T(8,128)} %vertex_in.1, ...), custom_call_target="tpu_custom_call" | custom-call | tf_op jit(solution)/shard_map/pallas_call | solution.py:446
  58.7 2.4 %copy.11 = f32[2,1,1,384,384]{4,3,2,1,0:T(8,128)} copy(f32[2,1,1,384,384]{4,3,2,1,0:T(8,128)} %shard_map.91) | data formatting | bytes 2359296

commit v3 on v2

--- a/solution.py
+++ b/solution.py
@@ -11,12 +11,11 @@
 LOWEST = -2.0
 SPREAD = 4.0
 CHUNK = 32
-MIX = 32
-ONE = 128
-PART = 32
+MIX = CHUNK
+ONE = 64
 WINDOW = 3
 LAG = 2
-GROUPS = (32, 96, 256)
+FIRST = 64
 F32 = jnp.float32
 BF16 = jnp.bfloat16
 
@@ -96,6 +95,7 @@
     one_ref,
     sum_ref,
     got_ref,
+    pair_ref,
     schur_send,
     schur_recv,
     x_send,
@@ -363,12 +363,13 @@
     def rows_of(c, size=CHUNK):
         return pl.ds(c * size, size)
 
+    def send_one(c):
+        at = rows_of(c)
+        pl.when(ahead)(lambda: one_copy(at, c * CHUNK // ONE).start())
+
     def send(c):
         x_copy(rows_of(c), c).start()
-        end = (c + 1) * CHUNK
-        if end % PART == 0:
-            at = pl.ds(end - PART, PART)
-            pl.when(ahead)(lambda: one_copy(at, (end - 1) // ONE).start())
+        send_one(c)
 
     th_ref[0], th_ref[1] = th, tl
 
@@ -377,18 +378,29 @@
         middle = dot3(al[0, at], al[1, at], th_ref[0], th_ref[1])
         g_ref[at] = av[at] + dot3(*split(middle), rr[0], rr[1])
 
-    start = 0
-    for rows in GROUPS:
-        apart(functools.partial(greens, start, rows))
-        for c in range(start // CHUNK, min((start + rows) // CHUNK, WINDOW)):
-            send(c)
-        start += rows
+    flipped = list(range(FIRST // CHUNK))
+    order = list(range(b // CHUNK, chunks)) + list(range(FIRST // CHUNK, b // CHUNK))
+    apart(functools.partial(greens, b, CHUNK))
+    send(order[0])
+    apart(functools.partial(greens, 0, FIRST))
+    for c in flipped:
+        raw = remote(g_ref.at[rows_of(c)], got_ref.at[rows_of(c)], sum_send, sum_recv.at[c], {"energy": sum_to})
+        pl.when(behind)(raw.start)
+        send_one(c)
+    apart(functools.partial(greens, b + CHUNK, r - CHUNK))
+    for c in order[1:WINDOW]:
+        send(c)
+    apart(functools.partial(greens, FIRST, b - FIRST))
+
+    def pair_copy(c):
+        return remote(pair_ref.at[rows_of(c)], x_ref.at[rows_of(c)], x_send, x_recv.at[c], {"energy": pair})
 
     def mix(start):
         at = slice(start, start + MIX)
-        mixed = w_pair * x_ref[at]
+        raw = start < FIRST
+        mixed = x_ref[at] if raw else w_pair * x_ref[at]
         mixed = mixed + jnp.where(behind, w_one * one_ref[at], 0.0)
-        mixed = mixed + jnp.where(ahead, got_ref[at], 0.0)
+        mixed = mixed + jnp.where(ahead, w_sum_own * got_ref[at] if raw else got_ref[at], 0.0)
         stacked = jnp.concatenate(
             [
                 jnp.concatenate([mixed[:, :b], mixed[:, 2 * b : 2 * b + r]], axis=1),
@@ -400,27 +412,41 @@
         for i, part in enumerate(split(dressed)):
             q[i, at, :n] = part[:MIX]
             q[i, at, n:] = part[MIX:]
-        if start + MIX == n - b:
-            early = slice(0, n - b)
+        if start + MIX == n:
+            early = slice(b, n)
             acc[...] = dot3(vp[0, :, early], vp[1, :, early], q[0, early], q[1, early])
 
-    for c in range(chunks + LAG):
-        if c < chunks:
+    seen = set()
+    for i in range(chunks + LAG):
+        if i < len(order):
+            c = order[i]
             x_copy(rows_of(c), c).wait_recv()
             at = slice(c * CHUNK, (c + 1) * CHUNK)
             sum_ref[at] = w_sum_own * g_ref[at] + w_sum_pair * x_ref[at]
             pl.when(behind)(lambda: sum_copy(rows_of(c), c).start())
-            if c + WINDOW < chunks:
-                send(c + WINDOW)
-        if c >= LAG:
-            done = c - LAG
-            if done * CHUNK % ONE == 0:
-                at = done * CHUNK // ONE
-                pl.when(behind)(lambda: one_copy(rows_of(at, ONE), at).wait_recv())
-            pl.when(ahead)(lambda: sum_copy(rows_of(done), done).wait_recv())
-            if (done + 1) * CHUNK % MIX == 0:
-                apart(functools.partial(mix, (done + 1) * CHUNK - MIX))
-    late = slice(n - b, n)
+            later = i + WINDOW
+            if later < len(order):
+                send(order[later])
+            elif later < chunks:
+                c = flipped[later - len(order)]
+                group = c * CHUNK // ONE
+                if group not in seen:
+                    seen.add(group)
+                    pl.when(behind)(lambda: one_copy(rows_of(group, ONE), group).wait_recv())
+                at = slice(c * CHUNK, (c + 1) * CHUNK)
+                pair_ref[at] = w_sum_pair * g_ref[at] + jnp.where(behind, w_pair * one_ref[at], 0.0)
+                pair_copy(c).start()
+        if i >= LAG:
+            c = (order + flipped)[i - LAG]
+            group = c * CHUNK // ONE
+            if group not in seen:
+                seen.add(group)
+                pl.when(behind)(lambda: one_copy(rows_of(group, ONE), group).wait_recv())
+            if c in flipped:
+                pair_copy(c).wait_recv()
+            pl.when(ahead)(lambda: sum_copy(rows_of(c), c).wait_recv())
+            apart(functools.partial(mix, c * CHUNK))
+    late = slice(0, b)
     stores = []
     for i in range(2):
         half = slice(i * n, (i + 1) * n)
@@ -477,6 +503,7 @@
             pltpu.VMEM((n, 2 * n), F32),
             pltpu.VMEM((n, 2 * n), F32),
             pltpu.VMEM((n, 2 * n), F32),
+            pltpu.VMEM((FIRST, 2 * n), F32),
             dma((3,)),
             dma((3,)),
             dma,

time: 61.2 us -> 58.8 us (0.961)
  Pallas kernels: 58.7 us -> 56.3 us
    pallas_call x1, Pallas kernels: 58.7 us -> 56.3 us  [per_device(): pl.pallas_call(kernel, out_shape=jax.ShapeDtypeStruct(arrays[5].shape, F3...]
where the time goes in v3:
time: 58.8 us; the launch traced here: 58.6 us
  Pallas kernels  56.3 us (96%)
  local copies, waits for them, and re-layouts  2.36 us (4%)
    pallas_call x1, Pallas kernels, per_device(): pl.pallas_call(kernel, out_shape=jax.ShapeDtypeStruct(arrays[5].shape, F3...  56.3 us
    unnamed x1, local copies, waits for them, and re-layouts  2.36 us

profile of v3, /device:TPU:24, one launch (start us, length us, event | category | flops | bytes accessed | tf_op | source)
XLA Modules:
  0.0 58.6 jit_solution(9293989199029154397)
XLA Ops:
  0.0 56.3 %shard_map.91 = f32[2,1,1,384,384]{4,3,2,1,0:T(8,128)} custom-call(f32[1,384]{1,0:T(1,128)} %onsite_in.1, f32[1,384,384]{2,1,0:T(8,128)} %hop_in.1, f32[128,128]{1,0:T(8,128)} %ham_in.1, f32[1,128]{1,0:T(1,128)} %cpl_in.1, s32[1,128]{1,0:T(1,128)} %bound_in.1, f32[2,1,1,384,384]{4,3,2,1,0:T(8,128)} %sigma_in.1, f32[1,384,384]{2,1,0:T(8,128)} %vertex_in.1, ...), custom_call_target="tpu_custom_call" | custom-call | tf_op jit(solution)/shard_map/pallas_call | solution.py:472
  56.3 2.4 %copy.11 = f32[2,1,1,384,384]{4,3,2,1,0:T(8,128)} copy(f32[2,1,1,384,384]{4,3,2,1,0:T(8,128)} %shard_map.91) | data formatting | bytes 2359296

commit v4 on v3

--- a/solution.py
+++ b/solution.py
@@ -199,7 +199,9 @@
     krh, krl = split(nr * dr - ni * di)
     kih, kil = split(nr * di + ni * dr)
     moved = dot(perm, jnp.concatenate([krh, kih, krl, kil], axis=1)).astype(BF16)
-    krh, kih, krl, kil = (dot(moved[:, i * n : (i + 1) * n], perm_t).astype(BF16) for i in range(4))
+    moved = jnp.concatenate([moved[:, i * n : (i + 1) * n] for i in range(4)], axis=0)
+    moved = dot(moved, perm_t).astype(BF16)
+    krh, kih, krl, kil = (moved[i * n : (i + 1) * n] for i in range(4))
     rows = iota((8, n), 0)
     pieces = jnp.zeros((8, n), F32)
     for i, d in enumerate((dr, di)):
@@ -239,9 +241,10 @@
         orbital = jnp.where(column < b, column, jnp.where((column >= 2 * b) & (column < 2 * b + r), column - b, -1))
         return jnp.where(row == orbital, 1.0, 0.0)
 
-    def y_rows(start, rows):
+    def y_rows(start, rows, k3=None):
         at = slice(start, start + rows)
-        k3 = dot3(khl[0, at], khl[1, at], rhs[0], rhs[1])
+        if k3 is None:
+            k3 = dot3(khl[0, at], khl[1, at], rhs[0], rhs[1])
         u = identity(start, rows) - khl[0, at].astype(F32) - khl[1, at].astype(F32) + yv[at] - k3
         y = dr_col[at] * u + di_col[at] * rot(u, b)
         yv[at] = y
@@ -253,13 +256,12 @@
         for i, part in enumerate(split(p)):
             store_rhs(k4r, i, part, turn(part), columns)
 
-    def k4_columns(columns, turn):
-        p = dot3(k2l[0], k2l[1], rhs[0, :, columns], rhs[1, :, columns])
-        for i, part in enumerate(split(p)):
-            store_rhs(k4r, i, part, turn(part), columns)
-
-    k4_columns(first, lambda part: rot(part, b))
-    y_rows(0, b)
+    stacked = [jnp.concatenate([khl[i, :b], k2l[i]], axis=0) for i in range(2)]
+    stacked = dot3(*stacked, rhs[0, :, first], rhs[1, :, first])
+    for i, part in enumerate(split(stacked[b:])):
+        store_rhs(k4r, i, part, rot(part, b), first)
+    k3 = dot3(khl[0, :b], khl[1, :b], rhs[0, :, rest], rhs[1, :, rest])
+    y_rows(0, b, jnp.concatenate([stacked[:b], k3], axis=1))
     corner = yv[:b, first] + dot3(yl[0, :b], yl[1, :b], k4r[0, :, first], k4r[1, :, first])
     loads[4].wait()
     c_row = cpl_ref[...]
@@ -331,8 +333,8 @@
     k2 = dot3(*kl, *turned(kl))
     k2s = split(k2)
     k2t = turned(k2s)
-    k3 = dot3(*kl, *k2t)
-    k4 = dot3(*k2s, *k2t)
+    both = dot3(*(jnp.concatenate(pieces, axis=0) for pieces in zip(kl, k2s)), *k2t)
+    k3, k4 = both[:b], both[b:]
     u = one - k + k2 - k3
     u = er_col * u + ei_col * rot(u, b)
     t = u + dot3(*split(u), *turned(split(k4)))

time: 58.8 us -> 58.7 us (level)
  no operation moved by 1% of the time
where the time goes in v4:
time: 58.7 us; the launch traced here: 58.6 us
  Pallas kernels  56.2 us (96%)
  local copies, waits for them, and re-layouts  2.36 us (4%)
    pallas_call x1, Pallas kernels, per_device(): pl.pallas_call(kernel, out_shape=jax.ShapeDtypeStruct(arrays[5].shape, F3...  56.2 us
    unnamed x1, local copies, waits for them, and re-layouts  2.36 us

profile of v4, /device:TPU:24, one launch (start us, length us, event | category | flops | bytes accessed | tf_op | source)
XLA Modules:
  0.0 58.6 jit_solution(8858214708946558483)
XLA Ops:
  0.0 56.2 %shard_map.91 = f32[2,1,1,384,384]{4,3,2,1,0:T(8,128)} custom-call(f32[1,384]{1,0:T(1,128)} %onsite_in.1, f32[1,384,384]{2,1,0:T(8,128)} %hop_in.1, f32[128,128]{1,0:T(8,128)} %ham_in.1, f32[1,128]{1,0:T(1,128)} %cpl_in.1, s32[1,128]{1,0:T(1,128)} %bound_in.1, f32[2,1,1,384,384]{4,3,2,1,0:T(8,128)} %sigma_in.1, f32[1,384,384]{2,1,0:T(8,128)} %vertex_in.1, ...), custom_call_target="tpu_custom_call" | custom-call | tf_op jit(solution)/shard_map/pallas_call | solution.py:474
  56.2 2.4 %copy.11 = f32[2,1,1,384,384]{4,3,2,1,0:T(8,128)} copy(f32[2,1,1,384,384]{4,3,2,1,0:T(8,128)} %shard_map.91) | data formatting | bytes 2359296

commit v5 on v4

--- a/solution.py
+++ b/solution.py
@@ -13,7 +13,7 @@
 CHUNK = 32
 MIX = CHUNK
 ONE = 64
-WINDOW = 3
+WINDOW = 4
 LAG = 2
 FIRST = 64
 F32 = jnp.float32

time: 58.7 us -> 58.7 us (level)
  no operation moved by 1% of the time
where the time goes in v5:
time: 58.7 us; the launch traced here: 58.6 us
  Pallas kernels  56.2 us (96%)
  local copies, waits for them, and re-layouts  2.36 us (4%)
    pallas_call x1, Pallas kernels, per_device(): pl.pallas_call(kernel, out_shape=jax.ShapeDtypeStruct(arrays[5].shape, F3...  56.2 us
    unnamed x1, local copies, waits for them, and re-layouts  2.36 us

profile of v5, /device:TPU:24, one launch (start us, length us, event | category | flops | bytes accessed | tf_op | source)
XLA Modules:
  0.0 58.6 jit_solution(6748083451360833839)
XLA Ops:
  0.0 56.2 %shard_map.91 = f32[2,1,1,384,384]{4,3,2,1,0:T(8,128)} custom-call(f32[1,384]{1,0:T(1,128)} %onsite_in.1, f32[1,384,384]{2,1,0:T(8,128)} %hop_in.1, f32[128,128]{1,0:T(8,128)} %ham_in.1, f32[1,128]{1,0:T(1,128)} %cpl_in.1, s32[1,128]{1,0:T(1,128)} %bound_in.1, f32[2,1,1,384,384]{4,3,2,1,0:T(8,128)} %sigma_in.1, f32[1,384,384]{2,1,0:T(8,128)} %vertex_in.1, ...), custom_call_target="tpu_custom_call" | custom-call | tf_op jit(solution)/shard_map/pallas_call | solution.py:474
  56.2 2.4 %copy.11 = f32[2,1,1,384,384]{4,3,2,1,0:T(8,128)} copy(f32[2,1,1,384,384]{4,3,2,1,0:T(8,128)} %shard_map.91) | data formatting | bytes 2359296

commit v6 on v4

--- a/solution.py
+++ b/solution.py
@@ -14,7 +14,7 @@
 MIX = CHUNK
 ONE = 64
 WINDOW = 3
-LAG = 2
+LAG = 3
 FIRST = 64
 F32 = jnp.float32
 BF16 = jnp.bfloat16

time: 58.7 us -> 58.7 us (level)
  no operation moved by 1% of the time
where the time goes in v6:
time: 58.7 us; the launch traced here: 58.6 us
  Pallas kernels  56.2 us (96%)
  local copies, waits for them, and re-layouts  2.36 us (4%)
    pallas_call x1, Pallas kernels, per_device(): pl.pallas_call(kernel, out_shape=jax.ShapeDtypeStruct(arrays[5].shape, F3...  56.2 us
    unnamed x1, local copies, waits for them, and re-layouts  2.36 us

profile of v6, /device:TPU:24, one launch (start us, length us, event | category | flops | bytes accessed | tf_op | source)
XLA Modules:
  0.0 58.6 jit_solution(14358101834878235724)
XLA Ops:
  0.0 56.2 %shard_map.91 = f32[2,1,1,384,384]{4,3,2,1,0:T(8,128)} custom-call(f32[1,384]{1,0:T(1,128)} %onsite_in.1, f32[1,384,384]{2,1,0:T(8,128)} %hop_in.1, f32[128,128]{1,0:T(8,128)} %ham_in.1, f32[1,128]{1,0:T(1,128)} %cpl_in.1, s32[1,128]{1,0:T(1,128)} %bound_in.1, f32[2,1,1,384,384]{4,3,2,1,0:T(8,128)} %sigma_in.1, f32[1,384,384]{2,1,0:T(8,128)} %vertex_in.1, ...), custom_call_target="tpu_custom_call" | custom-call | tf_op jit(solution)/shard_map/pallas_call | solution.py:474
  56.2 2.4 %copy.11 = f32[2,1,1,384,384]{4,3,2,1,0:T(8,128)} copy(f32[2,1,1,384,384]{4,3,2,1,0:T(8,128)} %shard_map.91) | data formatting | bytes 2359296
